TPU v7x, 128 devices: a whole 4x4x4 slice. The times are simulated.
128 devices in a mesh: row: 8 (over x_lo, z), col: 8 (over y, x_hi), head: 2 (over core).
Axes of the slice: x: 4 (x_hi: 2, x_lo: 2; x = x_hi * 2 + x_lo), y: 4, z: 4, core: 2. Of those that a mesh axis runs over, the one named last changes fastest.
Arguments:
- query_vectors: bfloat16 [8192, 768], P(('row', 'col'), 'head'), may hold values from -4.5 to 4.5
- key_vectors: bfloat16 [8192, 768], P(('row', 'col'), 'head'), may hold values from -4.5 to 4.5
- value_vectors: bfloat16 [8192, 768], P(('row', 'col'), 'head'), may hold values from -6 to 6
- segment_ids: int32 [8192], P(('row', 'col')), may hold values from 0 to 7, never falling along the last dimension, each value on 1 to 5120 neighbouring positions
- out_weight: bfloat16 [768, 1536], P('head'), may hold values from -0.21875 to 0.21875
- grad_output: bfloat16 [8192, 1536], P(('row', 'col')), may hold values from -6 to 6
Outputs:
- mixed_output: bfloat16 [8192, 1536], P(('row', 'col'))
- grad_queries: bfloat16 [8192, 768], P(('row', 'col'), 'head')
- grad_keys: bfloat16 [8192, 768], P(('row', 'col'), 'head')
- grad_values: bfloat16 [8192, 768], P(('row', 'col'), 'head')
Inputs may be any that keep to these rules, and one draw needn't show every extreme that they name: `segment_ids`: nondecreasing along the tokens; each of the 8 images holds 1 to 5120 tokens, and one holds exactly 5120.
All inputs are finite; a program needn't handle non-finite values.
Results may differ from a plain program's by a relative error of at most 0.019.
Values may be sent and summed in bfloat16 or wider, within the bound.
No kernel may reach another device: no remote copies, remote signals or barrier semaphores. Data moves between devices by JAX's collectives and lax.ppermute only.
A program may use at most 128 MiB of HBM per device.

v0:
```python
import math
import jax
import jax.numpy as jnp
from jax import lax
from jax.sharding import PartitionSpec as P

HD = 128


def score_scale():
    return 1.0 / math.sqrt(HD)


def split_heads(matrix):
    return matrix.reshape(matrix.shape[0], matrix.shape[1] // HD, HD)


def join_heads(stacked):
    return jnp.transpose(stacked, (1, 0, 2)).reshape(stacked.shape[1], -1)


def masked_scores(query_part, key_part, seg_query, seg_key):
    raw_scores = (
        jnp.einsum("qhd,khd->hqk", query_part, key_part, preferred_element_type=jnp.float32)
        * score_scale()
    )
    allowed = (seg_query[:, None] == seg_key[None, :])[None, :, :]
    return (jnp.where(allowed, raw_scores, -1e30), allowed)


def on_device(query_vectors, key_vectors, value_vectors, segment_ids, out_weight, grad_output):
    query_heads = split_heads(query_vectors)
    key_heads = split_heads(key_vectors)
    value_heads = split_heads(value_vectors)
    head_count = query_heads.shape[1]
    row_count = query_vectors.shape[0]
    grad_attn = jnp.einsum(
        "tw,cw->tc", grad_output, out_weight, preferred_element_type=jnp.float32
    ).astype(jnp.bfloat16)
    grad_heads = split_heads(grad_attn)
    start_max = jnp.full((head_count, row_count, 1), -1e30, jnp.float32)
    zero_stat = jnp.zeros((head_count, row_count, 1), jnp.float32)
    zero_accum = jnp.zeros((head_count, row_count, HD), jnp.float32)
    shard_piece = (
        lax.all_gather(key_vectors, ("row", "col"), axis=0, tiled=True),
        lax.all_gather(segment_ids, ("row", "col"), axis=0, tiled=True),
    )

    def update(current):
        running_max, running_sum = current
        scores, allowed = masked_scores(
            query_heads, split_heads(shard_piece[0]), segment_ids, shard_piece[-1]
        )
        new_max = jnp.maximum(running_max, jnp.max(scores, axis=2, keepdims=True))
        exp_terms = jnp.where(allowed, jnp.exp(scores - new_max), 0.0)
        running_sum = jnp.sum(exp_terms, axis=2, keepdims=True)
        return (new_max, running_sum)

    running_max, running_sum = update((start_max, zero_stat))
    log_norm = running_max + jnp.log(running_sum)
    make_shard_piece = (
        lax.all_gather(key_vectors, ("row", "col"), axis=0, tiled=True),
        lax.all_gather(value_vectors, ("row", "col"), axis=0, tiled=True),
        lax.all_gather(segment_ids, ("row", "col"), axis=0, tiled=True),
    )

    def update(current):
        key_part = split_heads(make_shard_piece[0])
        value_part = split_heads(make_shard_piece[1])
        scores, allowed = masked_scores(query_heads, key_part, segment_ids, make_shard_piece[2])
        prob_full = jnp.where(allowed, jnp.exp(scores - log_norm), 0.0)
        weights = prob_full.astype(jnp.bfloat16)
        grad_prob = jnp.einsum(
            "qhd,khd->hqk", grad_heads, value_part, preferred_element_type=jnp.float32
        )
        mix_weight = (prob_full * grad_prob).astype(jnp.bfloat16)
        acc_out = jnp.einsum(
            "hqk,khd->hqd", weights, value_part, preferred_element_type=jnp.float32
        )
        acc_mixed = jnp.einsum(
            "hqk,khd->hqd", mix_weight, key_part, preferred_element_type=jnp.float32
        )
        acc_plain = jnp.einsum(
            "hqk,khd->hqd", weights, key_part, preferred_element_type=jnp.float32
        )
        return (acc_out, acc_mixed, acc_plain)

    acc_out, acc_mixed, acc_plain = update((zero_accum, zero_accum, zero_accum))
    attn_heads = acc_out.astype(jnp.bfloat16)
    row_delta = jnp.einsum(
        "hqd,qhd->hq", attn_heads, grad_heads, preferred_element_type=jnp.float32
    )[:, :, None]
    query_grad = ((acc_mixed - row_delta * acc_plain) * score_scale()).astype(jnp.bfloat16)
    attn_rows = join_heads(attn_heads)
    partial_out = jnp.dot(attn_rows, out_weight, preferred_element_type=jnp.float32)
    mixed_output = lax.psum(partial_out.astype(jnp.bfloat16), "head")
    norm_rows = jnp.transpose(log_norm[:, :, 0])
    delta_rows = jnp.transpose(row_delta[:, :, 0])
    all_norms, all_deltas = (
        lax.all_gather(norm_rows, ("row", "col"), axis=0, tiled=True),
        lax.all_gather(delta_rows, ("row", "col"), axis=0, tiled=True),
    )
    zero_keys = jnp.zeros((row_count, head_count, HD), jnp.float32)
    query_piece = lax.all_gather(query_vectors, ("row", "col"), axis=0, tiled=True)
    grad_piece = lax.all_gather(grad_attn, ("row", "col"), axis=0, tiled=True)
    seg_piece = lax.all_gather(segment_ids, ("row", "col"), axis=0, tiled=True)

    def update(current):
        query_part = split_heads(query_piece)
        grad_part = split_heads(grad_piece)
        norm_part = jnp.transpose(all_norms)[:, :, None]
        delta_part = jnp.transpose(all_deltas)[:, :, None]
        scores, allowed = masked_scores(query_part, key_heads, seg_piece, segment_ids)
        prob_full = jnp.where(allowed, jnp.exp(scores - norm_part), 0.0)
        weights = prob_full.astype(jnp.bfloat16)
        grad_prob = jnp.einsum(
            "qhd,khd->hqk", grad_part, value_heads, preferred_element_type=jnp.float32
        )
        grad_scores = (prob_full * (grad_prob - delta_part) * score_scale()).astype(jnp.bfloat16)
        acc_key = jnp.einsum(
            "hqk,qhd->khd", grad_scores, query_part, preferred_element_type=jnp.float32
        )
        acc_value = jnp.einsum(
            "hqk,qhd->khd", weights, grad_part, preferred_element_type=jnp.float32
        )
        return (acc_key, acc_value)

    acc_key, acc_value = update((zero_keys, zero_keys))
    grad_keys = acc_key.reshape(row_count, -1).astype(jnp.bfloat16)
    grad_values = acc_value.reshape(row_count, -1).astype(jnp.bfloat16)
    grad_queries = join_heads(query_grad)
    return (mixed_output, grad_queries, grad_keys, grad_values)


def solution(mesh):
    in_specs = (
        P(("row", "col"), "head"),
        P(("row", "col"), "head"),
        P(("row", "col"), "head"),
        P(("row", "col")),
        P("head", None),
        P(("row", "col"), None),
    )
    out_specs = (
        P(("row", "col"), None),
        P(("row", "col"), "head"),
        P(("row", "col"), "head"),
        P(("row", "col"), "head"),
    )
    return jax.shard_map(
        on_device, mesh=mesh, in_specs=in_specs, out_specs=out_specs, check_vma=False
    )
```

profile of v0, /device:TPU:0, one launch (start us, length us, event | category | flops | bytes accessed | tf_op | source)
XLA Modules:
  0.0 1367.7 jit_solution(1729225022353792383)
XLA Ops:
  8.0 1.6 copy.36
  9.7 1.6 copy.35
  11.4 2.1 convolution_convert_fusion.2
  14.6 1.7 copy.48
  16.3 177.8 %all-gather = s32[64,1,128]{2,1,0:T(1,128)S(1)} all-gather(s32[1,1,128]{2,1,0:T(1,128)} %bitcast.78), channel_id=1, replica_groups=mesh['row'=8,'col'=8,'head'=2] {'row','col'}, dimensions={0}, use_global_device_ids=true | all-gather | bytes 33280 | tf_op jit(solution)/shard_map/all_gather | solution.py:64
  194.1 1.3 broadcast_compare_fusion.1
  195.4 4.4 broadcast_compare_fusion
  199.9 156.8 %all-gather.8.cloned.1.call-done = bf16[8192,384]{1,0:T(8,128)(2,1)} async-done(((bf16[128,384]{1,0:T(8,128)(2,1)}), bf16[8192,384]{1,0:T(8,128)(2,1)}) %all-gather.8.cloned.1.call-update) | async-done | bytes 6291472 | tf_op jit(solution)/shard_map/all_gather | solution.py:63
  356.7 8.7 copy.39
  365.3 301.0 %all-gather.6.cloned.1.call-done = bf16[8192,384]{0,1:T(8,128)(2,1)} async-done(((bf16[128,384]{0,1:T(8,128)(2,1)}), bf16[8192,384]{0,1:T(8,128)(2,1)}) %all-gather.6.cloned.1.call-update) | async-done | bytes 6291472 | tf_op jit(solution)/shard_map/all_gather | solution.py:62
  666.4 10.5 fusion.17
  676.9 7.6 select_reduce_fusion
  684.5 176.8 %all_gather.28 = f32[8192,3]{0,1:T(4,128)S(1)} all-gather(f32[128,3]{0,1:T(4,128)S(1)} %bitcast.77), channel_id=1, replica_groups=mesh['row'=8,'col'=8,'head'=2] {'row','col'}, dimensions={0}, use_global_device_ids=true | all-gather | bytes 99840 | tf_op jit(solution)/shard_map/all_gather | solution.py:100
  861.3 9.6 fusion.12
  870.9 171.9 %all_gather.30 = f32[8192,3]{0,1:T(4,128)S(1)} all-gather(f32[128,3]{0,1:T(4,128)S(1)} %get-tuple-element.18), channel_id=1, replica_groups=mesh['row'=8,'col'=8,'head'=2] {'row','col'}, dimensions={0}, use_global_device_ids=true | all-gather | bytes 99840 | tf_op jit(solution)/shard_map/all_gather | solution.py:101
  1042.8 2.0 convolution_convert_fusion
  1044.9 12.0 convolution_bitcast_fusion.1
  1056.9 9.6 fusion.9
  1066.5 10.2 exponential_select_fusion
  1076.7 252.3 %all-gather.12.cloned.1.call-done = bf16[8192,384]{1,0:T(8,128)(2,1)} async-done(((bf16[128,384]{1,0:T(8,128)(2,1)}), bf16[8192,384]{1,0:T(8,128)(2,1)}) %all-gather.12.cloned.1.call-update) | async-done | bytes 6291472 | tf_op jit(solution)/shard_map/all_gather | solution.py:105
  1329.0 8.7 copy.47
  1337.7 10.9 convolution_convert_fusion.1
  1348.7 8.5 fusion.6
  1359.4 1.8 copy.70
  (32 shorter events, 4.3 us)
Async XLA Ops:
  7.2 4.2 copy-start
  7.2 349.5 %all-gather.8.cloned.1.call-start = ((), (), s32[]{:S(2)}) async-start(), calls=%async_computation.1 | async-start | bytes 6389760 | tf_op jit(solution)/shard_map/all_gather | solution.py:63
  7.9 658.5 %all-gather.6.cloned.1.call-start = ((), (), s32[]{:S(2)}) async-start(), calls=%async_computation | async-start | bytes 6389760 | tf_op jit(solution)/shard_map/all_gather | solution.py:62
  9.6 1056.9 %all-gather.10.cloned.1.call-start = ((), (), s32[]{:S(2)}) async-start(), calls=%async_computation.3 | async-start | bytes 6389760 | tf_op jit(solution)/shard_map/all_gather | solution.py:104
  11.3 1317.7 %all-gather.12.cloned.1.call-start = ((), (), s32[]{:S(2)}) async-start(), calls=%async_computation.4 | async-start | bytes 6389760 | tf_op jit(solution)/shard_map/all_gather | solution.py:105
  13.6 1345.9 %all-reduce.2.cloned.1.call-start = ((), (), s32[]{:S(2)}) async-start(), calls=%async_computation.2 | async-start | bytes 786432 | tf_op jit(solution)/shard_map/psum | solution.py:96
  14.6 846.7 %copy-start.5 = (bf16[128,384]{0,1:T(8,128)(2,1)}, bf16[128,384]{0,1:T(8,128)(2,1)S(1)}, u32[]{:S(2)}) copy-start(bf16[128,384]{0,1:T(8,128)(2,1)S(1)} %copy.40) | copy-start | bytes 294916
  199.8 466.5 %copy-start.2 = (bf16[128,384]{0,1:T(8,128)(2,1)S(1)}, bf16[128,384]{0,1:T(8,128)(2,1)}, u32[]{:S(2)}) copy-start(bf16[128,384]{0,1:T(8,128)(2,1)} %copy.35) | copy-start | bytes 294916
  1056.9 9.7 copy-start.4
  1076.7 261.0 %copy-start.3 = (bf16[128,384]{0,1:T(8,128)(2,1)S(1)}, bf16[128,384]{0,1:T(8,128)(2,1)}, u32[]{:S(2)}) copy-start(bf16[128,384]{0,1:T(8,128)(2,1)} %copy.48) | copy-start | bytes 294916
  1348.7 8.5 copy-start.6
  1348.7 12.5 copy-start.1
Sparse Core Ops, SparseCore 0:
  9.7 346.9 all-gather.7
  358.8 307.5 all-gather.5
  668.5 314.5 all-gather.9
  985.2 343.7 all-gather.11
  1331.9 21.4 all-reduce.1
where the time goes:
time: 1370 us
  waiting for transfers between devices  711 us (52%)
  blocking collectives  527 us (38%)
  matrix products  75.5 us (6%)
  local copies, waits for them, and re-layouts  27.4 us (2%)
  between operations  13.9 us (1%)
    all_gather x1, waiting for transfers between devices, on_device(): lax.all_gather(key_vectors, ('row', 'col'), axis=0, tiled=True)  301 us
    all_gather x1, waiting for transfers between devices, on_device(): grad_piece = lax.all_gather(grad_attn, ('row', 'col'), axis=0, tiled=True)  252 us
    all_gather x1, blocking collectives, on_device(): lax.all_gather(segment_ids, ('row', 'col'), axis=0, tiled=True)  178 us
    all_gather x1, blocking collectives, on_device(): lax.all_gather(norm_rows, ('row', 'col'), axis=0, tiled=True)  177 us
    all_gather x1, blocking collectives, on_device(): lax.all_gather(delta_rows, ('row', 'col'), axis=0, tiled=True)  172 us
    all_gather x1, waiting for transfers between devices, on_device(): lax.all_gather(value_vectors, ('row', 'col'), axis=0, tiled=True)  157 us
  transfers between devices with their start and end apart: 5, of which 3 were waited for; matrix products, arithmetic and copies ran while one was open for 8% of the time, Pallas kernels for 0%

commit v1 on v0

--- a/solution.py
+++ b/solution.py
@@ -60,7 +60,12 @@
     log_norm = running_max + jnp.log(running_sum)
     make_shard_piece = (
         lax.all_gather(key_vectors, ("row", "col"), axis=0, tiled=True),
-        lax.all_gather(value_vectors, ("row", "col"), axis=0, tiled=True),
+        jnp.concatenate(
+            lax.all_to_all(
+                jnp.stack([value_vectors] * lax.axis_size(("row", "col"))), ("row", "col"), 0, 0
+            ),
+            axis=0,
+        ),
         lax.all_gather(segment_ids, ("row", "col"), axis=0, tiled=True),
     )
 

time: 1370 us -> 1060 us (0.77)
  waiting for transfers between devices: 711 us -> 291 us
  blocking collectives: 527 us -> 613 us
  local copies, waits for them, and re-layouts: 27.4 us -> 42.2 us
    all_gather x1, waiting for transfers between devices: 301 us -> 41.7 us  [on_device(): lax.all_gather(key_vectors, ('row', 'col'), axis=0, tiled=True)]
    all_gather x1 -> x0, waiting for transfers between devices: 157 us -> none  [on_device(): lax.all_gather(value_vectors, ('row', 'col'), axis=0, tiled=True)]
    all_gather x1, blocking collectives: 178 us -> 263 us  [on_device(): lax.all_gather(segment_ids, ('row', 'col'), axis=0, tiled=True)]
    another operation x0 -> x2, local copies, waits for them, and re-layouts: none -> 14.5 us  [the longest x1 10.4 us: split_heads(): return matrix.reshape(matrix.shape[0], matrix.shape[1] // HD, HD)]
  transfers between devices with their start and end apart: 5 -> 5, of which waited for: 3 -> 2; matrix products, arithmetic and copies ran while one was open for 8% -> 12% of each run, Pallas kernels for 0% -> 0%
where the time goes in v1:
time: 1060 us
  blocking collectives  613 us (58%)
  waiting for transfers between devices  291 us (27%)
  matrix products  74.9 us (7%)
  local copies, waits for them, and re-layouts  42.2 us (4%)
  between operations  13.9 us (1%)
  other arithmetic  12.1 us (1%)
  starting transfers between devices  12 us (1%)
    all_gather x1, blocking collectives, on_device(): lax.all_gather(segment_ids, ('row', 'col'), axis=0, tiled=True)  263 us
    all_gather x1, waiting for transfers between devices, on_device(): grad_piece = lax.all_gather(grad_attn, ('row', 'col'), axis=0, tiled=True)  249 us
    all_gather x1, blocking collectives, on_device(): lax.all_gather(norm_rows, ('row', 'col'), axis=0, tiled=True)  177 us
    all_gather x1, blocking collectives, on_device(): lax.all_gather(delta_rows, ('row', 'col'), axis=0, tiled=True)  173 us
    all_gather x1, waiting for transfers between devices, on_device(): lax.all_gather(key_vectors, ('row', 'col'), axis=0, tiled=True)  41.7 us
  transfers between devices with their start and end apart: 5, of which 2 were waited for; matrix products, arithmetic and copies ran while one was open for 12% of the time, Pallas kernels for 0%

profile of v1, /device:TPU:0, one launch (start us, length us, event | category | flops | bytes accessed | tf_op | source)
XLA Modules:
  0.0 1059.3 jit_solution(3901567851399499991)
XLA Ops:
  7.2 1.7 copy.36
  9.0 1.6 copy.35
  11.7 4.2 stack.2
  15.9 11.9 %all-to-all-start = ((bf16[64,128,384]{1,2,0:T(8,128)(2,1)}), bf16[64,128,384]{1,2,0:T(8,128)(2,1)}, u32[]{:S(2)}, u32[]{:S(2)}) async-start(bf16[64,128,384]{1,2,0:T(8,128)(2,1)} %stack.2), calls=%async_computation | async-start | bytes 12582912 | tf_op jit(solution)/shard_map/all_to_all | solution.py:64
  27.8 1.2 convolution_convert_fusion.2
  30.1 263.4 %all-gather = s32[64,1,128]{2,1,0:T(1,128)S(1)} all-gather(s32[1,1,128]{2,1,0:T(1,128)S(1)} %bitcast.77), channel_id=1, replica_groups=mesh['row'=8,'col'=8,'head'=2] {'row','col'}, dimensions={0}, use_global_device_ids=true | all-gather | bytes 33280 | tf_op jit(solution)/shard_map/all_gather | solution.py:69
  294.1 3.9 broadcast_compare_fusion
  298.1 9.5 copy.40
  307.6 10.4 reshape_reshape.3
  317.9 41.7 %all-gather.5.cloned.1.call-done = bf16[8192,384]{0,1:T(8,128)(2,1)} async-done(((bf16[128,384]{0,1:T(8,128)(2,1)}), bf16[8192,384]{0,1:T(8,128)(2,1)}) %all-gather.5.cloned.1.call-update) | async-done | bytes 6291472 | tf_op jit(solution)/shard_map/all_gather | solution.py:62
  359.6 10.5 fusion.17
  370.1 7.6 select_reduce_fusion
  377.7 177.2 %all_gather.24 = f32[8192,3]{0,1:T(4,128)S(1)} all-gather(f32[128,3]{0,1:T(4,128)S(1)} %bitcast.76), channel_id=1, replica_groups=mesh['row'=8,'col'=8,'head'=2] {'row','col'}, dimensions={0}, use_global_device_ids=true | all-gather | bytes 99840 | tf_op jit(solution)/shard_map/all_gather | solution.py:105
  554.9 9.6 fusion.12
  564.5 172.5 %all_gather.26 = f32[8192,3]{0,1:T(4,128)S(1)} all-gather(f32[128,3]{0,1:T(4,128)S(1)} %get-tuple-element.18), channel_id=1, replica_groups=mesh['row'=8,'col'=8,'head'=2] {'row','col'}, dimensions={0}, use_global_device_ids=true | all-gather | bytes 99840 | tf_op jit(solution)/shard_map/all_gather | solution.py:106
  737.1 2.0 convolution_convert_fusion
  739.1 12.2 %convolution_bitcast_fusion.1 = f32[128,3,128]{0,2,1:T(8,128)S(1)} fusion(bf16[8192,3,128]{0,2,1:T(8,128)(2,1)} %bitcast.61, bf16[128,3,128]{0,2,1:T(8,128)(2,1)} %bitcast.74, bf16[8192,3,128]{0,2,1:T(8,128)(2,1)} %reshape_reshape.3, f32[3,128,8192]{2,1,0:T(8,128)} %get-tuple-element.17, f32[3,128]{1,0:T(4,128)S(1)} %log_add_fusion, ...), kind=kOutput, calls=%fused_computation.14 | convolution fusion | flops 1623195648 | bytes 26510848 | tf_op jit(solution)/shard_map/hqk,khd->hqd/dot_general | solution.py:85
  751.3 9.6 fusion.9
  761.0 10.2 exponential_select_fusion
  771.2 249.3 %all-gather.9.cloned.1.call-done = bf16[8192,384]{1,0:T(8,128)(2,1)} async-done(((bf16[128,384]{1,0:T(8,128)(2,1)}), bf16[8192,384]{1,0:T(8,128)(2,1)}) %all-gather.9.cloned.1.call-update) | async-done | bytes 6291472 | tf_op jit(solution)/shard_map/all_gather | solution.py:110
  1020.5 8.7 copy.48
  1029.2 11.0 %convolution_convert_fusion.1 = bf16[3,128,128]{1,2,0:T(8,128)(2,1)S(1)} fusion(bf16[8192,3,128]{0,2,1:T(8,128)(2,1)} %bitcast.59, f32[3,8192,128]{2,1,0:T(8,128)} %exponential_select_fusion, bf16[8192,3,128]{0,2,1:T(8,128)(2,1)} %bitcast.56, bf16[128,3,128]{0,2,1:T(8,128)(2,1)S(1)} %bitcast.65, f32[3,8192]{1,0:T(4,128)S(1)} %bitcast.63), kind=kOutput, calls=%fused_computation.18 | convolution fusion | flops 1623244800 | bytes 25460736 | tf_op jit(solution)/shard_map/hqk,qhd->khd/dot_general | solution.py:125
  1040.2 8.5 fusion.6
  1051.0 1.8 copy.71
  (39 shorter events, 5.2 us)
Async XLA Ops:
  7.2 20.6 %copy-start = (bf16[384,1536]{1,0:T(8,128)(2,1)S(1)}, bf16[384,1536]{1,0:T(8,128)(2,1)}, u32[]{:S(2)}) copy-start(bf16[384,1536]{1,0:T(8,128)(2,1)} %param.10) | copy-start | bytes 3538948
  7.2 352.4 %all-gather.5.cloned.1.call-start = ((), (), s32[]{:S(2)}) async-start(), calls=%async_computation.1 | async-start | bytes 6389760 | tf_op jit(solution)/shard_map/all_gather | solution.py:62
  9.0 752.0 %all-gather.7.cloned.1.call-start = ((), (), s32[]{:S(2)}) async-start(), calls=%async_computation.3 | async-start | bytes 6389760 | tf_op jit(solution)/shard_map/all_gather | solution.py:109
  11.7 4.2 copy-start.3
  15.9 11.9 %copy-start.6 = (bf16[128,1536]{1,0:T(8,128)(2,1)S(1)}, bf16[128,1536]{1,0:T(8,128)(2,1)}, u32[]{:S(2)}) copy-start(bf16[128,1536]{1,0:T(8,128)(2,1)} %param.11) | copy-start | bytes 1179652
  15.9 14.2 %copy-start.9 = (s32[128]{0:T(128)S(1)}, s32[128]{0:T(128)}, u32[]{:S(2)}) copy-start(s32[128]{0:T(128)} %param.9) | copy-start | bytes 1540
  15.9 282.2 %all-to-all-start = ((bf16[64,128,384]{1,2,0:T(8,128)(2,1)}), bf16[64,128,384]{1,2,0:T(8,128)(2,1)}, u32[]{:S(2)}, u32[]{:S(2)}) async-start(bf16[64,128,384]{1,2,0:T(8,128)(2,1)} %stack.2), calls=%async_computation | async-start | bytes 12582912 | tf_op jit(solution)/shard_map/all_to_all | solution.py:64
  27.8 992.7 %all-gather.9.cloned.1.call-start = ((), (), s32[]{:S(2)}) async-start(), calls=%async_computation.4 | async-start | bytes 6389760 | tf_op jit(solution)/shard_map/all_gather | solution.py:110
  29.0 1022.0 %all-reduce.2.cloned.1.call-start = ((), (), s32[]{:S(2)}) async-start(), calls=%async_computation.2 | async-start | bytes 786432 | tf_op jit(solution)/shard_map/psum | solution.py:101
  30.1 524.8 %copy-start.7 = (bf16[128,384]{0,1:T(8,128)(2,1)}, bf16[128,384]{0,1:T(8,128)(2,1)S(1)}, u32[]{:S(2)}) copy-start(bf16[128,384]{0,1:T(8,128)(2,1)S(1)} %copy.41) | copy-start | bytes 294916
  307.6 52.0 %copy-start.2 = (bf16[128,384]{0,1:T(8,128)(2,1)S(1)}, bf16[128,384]{0,1:T(8,128)(2,1)}, u32[]{:S(2)}) copy-start(bf16[128,384]{0,1:T(8,128)(2,1)} %copy.35) | copy-start | bytes 294916
  751.3 9.7 copy-start.5
  771.2 258.0 %copy-start.4 = (bf16[128,384]{0,1:T(8,128)(2,1)S(1)}, bf16[128,384]{0,1:T(8,128)(2,1)}, u32[]{:S(2)}) copy-start(bf16[128,384]{0,1:T(8,128)(2,1)} %copy-done.3) | copy-start | bytes 294916
  1040.2 8.5 copy-start.8
  1040.2 12.6 %copy-start.1 = (bf16[384,1536]{1,0:T(8,128)(2,1)S(1)}, bf16[384,1536]{1,0:T(8,128)(2,1)}, u32[]{:S(2)}) copy-start(bf16[384,1536]{1,0:T(8,128)(2,1)} %param.10) | copy-start | bytes 3538948
Sparse Core Ops, SparseCore 0:
  10.2 349.4 all-gather.4
  361.7 313.8 all-gather.6
  677.9 342.5 all-gather.8
  1023.3 21.9 all-reduce.1
